TPU v7x, 32 devices: a whole 2x2x4 slice. The times are simulated.
32 devices in a mesh: level: 4 (over y, x), req: 8 (over z, core).
Axes of the slice: x: 2, y: 2, z: 4, core: 2. Of those that a mesh axis runs over, the one named last changes fastest.
Arguments:
- queries: bfloat16 [256, 64, 896], P('level', 'req'), may hold values from -120 to 120
- out_grad: bfloat16 [256, 64, 896], P('level', 'req'), may hold values from -5 to 5
- resp_key: bfloat16 [256, 64, 128], P('level', 'req'), may hold values from -4 to 4
- resp_value: bfloat16 [256, 64, 128], P('level', 'req'), may hold values from -4 to 4
- sys_key: bfloat16 [128, 128], P('level'), may hold values from -4 to 4
- sys_value: bfloat16 [128, 128], P('level'), may hold values from -4 to 4
- ctx_key: bfloat16 [16, 128, 128], P('req', 'level'), may hold values from -4 to 4
- ctx_value: bfloat16 [16, 128, 128], P('req', 'level'), may hold values from -4 to 4
- parent: int32 [64], P('req'), may hold values from 0 to 15, as said below
- resp_len: int32 [64], P('req'), may hold values from 64 to 256
- ctx_len: int32 [16], P('req'), may hold values from 32 to 128
Outputs:
- d_queries: float32 [256, 64, 896], P('level', 'req')
- d_sys_key: float32 [128, 128], P(('level', 'req'))
- d_sys_value: float32 [128, 128], P(('level', 'req'))
- d_ctx_key: float32 [16, 128, 128], P('req', 'level')
- d_ctx_value: float32 [16, 128, 128], P('req', 'level')
- d_resp_key: float32 [256, 64, 128], P('level', 'req')
- d_resp_value: float32 [256, 64, 128], P('level', 'req')
Inputs may be any that keep to these rules, and one draw needn't show every extreme that they name: Response i's parent is one of the contexts (i // 8) * 2 to (i // 8 + 1) * 2 - 1.
All inputs are finite; a program needn't handle non-finite values.
Results may differ from a plain program's by a relative error of at most 0.0049.
Values may be sent and summed in bfloat16 or wider, within the bound.
A program may use at most 64 MiB of HBM per device.

v0:
```python
import jax
import jax.numpy as jnp
from jax import lax
from jax.sharding import PartitionSpec as P

HEADS = 7
HEAD_DIM = 128
CTX_PER = 2


NEGATIVE = -1e30
HIGHEST = lax.Precision.HIGHEST


def stacked(key_rows, block_width):
    count = key_rows.shape[1] // block_width
    return jnp.swapaxes(
        key_rows.reshape(key_rows.shape[0], count, block_width, key_rows.shape[2]), 0, 1
    )


def allowed_mask(block_start, block_width, limits, causal, row_places):
    places = block_start + jnp.arange(block_width, dtype=jnp.int32)
    allowed = places[None, :, None, None] < limits[:, None, None, None]
    if causal:
        allowed = allowed & (places[None, :, None, None] <= row_places[None, None, None, :])
    return allowed


def block_scores(key_block, queries_all):
    return jnp.einsum(
        "rkd,trhd->rkht", key_block, queries_all, preferred_element_type=jnp.float32
    ) * HEAD_DIM ** (-0.5)


def forward_segment(
    partials, key_rows, value_rows, limits, causal, row_places, queries_all, grads_all
):
    block_width = min(128, key_rows.shape[1])
    starts = block_width * jnp.arange(key_rows.shape[1] // block_width, dtype=jnp.int32)

    def forward_advance(carried, pieces):
        key_block, value_block, block_start = pieces
        maxima, totals, running = carried
        allowed = allowed_mask(block_start, block_width, limits, causal, row_places)
        scores = block_scores(key_block, queries_all)
        new_max = jnp.maximum(maxima, jnp.max(jnp.where(allowed, scores, NEGATIVE), axis=1))
        weights = jnp.where(allowed, jnp.exp(scores - new_max[:, None]), 0.0)
        shrink = jnp.exp(maxima - new_max)
        totals = shrink * totals + jnp.sum(weights, axis=1)
        products = jnp.einsum(
            "rkd,trhd->rkht", value_block, grads_all, preferred_element_type=jnp.float32
        )
        running = shrink * running + jnp.sum(weights * products, axis=1)
        return ((new_max, totals, running), None)

    partials, unused = lax.scan(
        forward_advance,
        partials,
        (stacked(key_rows, block_width), stacked(value_rows, block_width), starts),
    )
    return partials


def backward_segment(
    query_sum,
    key_rows,
    value_rows,
    limits,
    causal,
    row_places,
    queries_all,
    grads_all,
    logsum,
    deltas,
    shared,
):
    block_width = min(128, key_rows.shape[1])
    starts = block_width * jnp.arange(key_rows.shape[1] // block_width, dtype=jnp.int32)
    scaling = HEAD_DIM ** (-0.5)
    grad_form = "rkht,trhd->kd" if shared else "rkht,trhd->rkd"

    def backward_advance(carried, pieces):
        key_block, value_block, block_start = pieces
        allowed = allowed_mask(block_start, block_width, limits, causal, row_places)
        scores = block_scores(key_block, queries_all)
        chances = jnp.where(allowed, jnp.exp(scores - logsum[:, None]), 0.0)
        products = jnp.einsum(
            "rkd,trhd->rkht", value_block, grads_all, preferred_element_type=jnp.float32
        )
        slopes = (chances * (products - deltas[:, None])).astype(jnp.bfloat16)
        carried = carried + scaling * jnp.einsum(
            "rkht,rkd->trhd", slopes, key_block, preferred_element_type=jnp.float32
        )
        key_grad = scaling * jnp.einsum(
            grad_form, slopes, queries_all, preferred_element_type=jnp.float32
        )
        value_grad = jnp.einsum(
            grad_form, chances.astype(jnp.bfloat16), grads_all, preferred_element_type=jnp.float32
        )
        return (carried, (key_grad, value_grad))

    query_sum, grads_pair = lax.scan(
        backward_advance,
        query_sum,
        (stacked(key_rows, block_width), stacked(value_rows, block_width), starts),
    )
    if shared:
        key_grads = grads_pair[0].reshape(key_rows.shape[1], key_rows.shape[2])
        value_grads = grads_pair[1].reshape(key_rows.shape[1], key_rows.shape[2])
    else:
        key_grads = jnp.swapaxes(grads_pair[0], 0, 1).reshape(key_rows.shape)
        value_grads = jnp.swapaxes(grads_pair[1], 0, 1).reshape(value_rows.shape)
    return (query_sum, key_grads, value_grads)


def shards(
    queries,
    out_grad,
    resp_key,
    resp_value,
    sys_key,
    sys_value,
    ctx_key,
    ctx_value,
    parent,
    resp_len,
    ctx_len,
):
    sys_keys, sys_values, ctx_keys_all, ctx_values_all, own_keys, own_values = (
        lax.all_gather(sys_key, "level", axis=0, tiled=True),
        lax.all_gather(sys_value, "level", axis=0, tiled=True),
        lax.all_gather(ctx_key, "level", axis=1, tiled=True),
        lax.all_gather(ctx_value, "level", axis=1, tiled=True),
        lax.all_gather(resp_key, "level", axis=0, tiled=True),
        lax.all_gather(resp_value, "level", axis=0, tiled=True),
    )
    length = queries.shape[0]
    responses = queries.shape[1]
    row_places = lax.axis_index("level") * length + jnp.arange(length, dtype=jnp.int32)
    queries_all = queries.reshape(length, responses, HEADS, HEAD_DIM)
    live_rows = row_places[:, None] < resp_len[None, :]
    grads_all = jnp.where(
        live_rows[:, :, None, None],
        out_grad.reshape(length, responses, HEADS, HEAD_DIM),
        jnp.zeros((), jnp.bfloat16),
    )
    local_parent = parent - lax.axis_index("req") * CTX_PER
    choose = local_parent[:, None] == jnp.arange(CTX_PER, dtype=jnp.int32)[None, :]
    choose_low = choose.astype(jnp.bfloat16)
    choose_float = choose.astype(jnp.float32)
    ctx_limits = jnp.sum(jnp.where(choose, ctx_len[None, :], 0), axis=1)
    ctx_keys = jnp.einsum(
        "rc,cnd->rnd", choose_low, ctx_keys_all, preferred_element_type=jnp.float32
    ).astype(jnp.bfloat16)
    ctx_values = jnp.einsum(
        "rc,cnd->rnd", choose_low, ctx_values_all, preferred_element_type=jnp.float32
    ).astype(jnp.bfloat16)
    sys_keys = jnp.broadcast_to(sys_keys[None], (responses,) + sys_keys.shape)
    sys_values = jnp.broadcast_to(sys_values[None], (responses,) + sys_values.shape)
    own_keys = jnp.swapaxes(own_keys, 0, 1)
    own_values = jnp.swapaxes(own_values, 0, 1)
    open_limits = jnp.full((responses,), 2**30, jnp.int32)
    segments = [
        (sys_keys, sys_values, open_limits, False, True),
        (ctx_keys, ctx_values, ctx_limits, False, False),
        (own_keys, own_values, open_limits, True, False),
    ]
    maxima = jnp.full((responses, HEADS, length), NEGATIVE, jnp.float32)
    totals = jnp.zeros((responses, HEADS, length), jnp.float32)
    running = jnp.zeros((responses, HEADS, length), jnp.float32)
    partials = (maxima, totals, running)
    for key_rows, value_rows, limits, causal, shared in segments:
        partials = forward_segment(
            partials, key_rows, value_rows, limits, causal, row_places, queries_all, grads_all
        )
    maxima, totals, running = partials
    deltas = running / totals
    logsum = maxima + jnp.log(totals)
    query_sum = jnp.zeros((length, responses, HEADS, HEAD_DIM), jnp.float32)
    results = []
    for key_rows, value_rows, limits, causal, shared in segments:
        query_sum, key_grads, value_grads = backward_segment(
            query_sum,
            key_rows,
            value_rows,
            limits,
            causal,
            row_places,
            queries_all,
            grads_all,
            logsum,
            deltas,
            shared,
        )
        results.append((key_grads, value_grads))
    sys_kpart, sys_vpart = results[0]
    ctx_kpart = jnp.einsum("rc,rnd->ncd", choose_float, results[1][0], precision=HIGHEST)
    ctx_vpart = jnp.einsum("rc,rnd->ncd", choose_float, results[1][1], precision=HIGHEST)
    own_kpart = jnp.swapaxes(results[2][0], 0, 1)
    own_vpart = jnp.swapaxes(results[2][1], 0, 1)
    ctx_kgrad, ctx_vgrad, own_kgrad, own_vgrad = (
        lax.psum_scatter(ctx_kpart, "level", scatter_dimension=0, tiled=True),
        lax.psum_scatter(ctx_vpart, "level", scatter_dimension=0, tiled=True),
        lax.psum_scatter(own_kpart, "level", scatter_dimension=0, tiled=True),
        lax.psum_scatter(own_vpart, "level", scatter_dimension=0, tiled=True),
    )
    sys_kgrad, sys_vgrad = (
        lax.psum_scatter(sys_kpart, ("level", "req"), scatter_dimension=0, tiled=True),
        lax.psum_scatter(sys_vpart, ("level", "req"), scatter_dimension=0, tiled=True),
    )
    d_ctx_key = jnp.swapaxes(ctx_kgrad, 0, 1)
    d_ctx_value = jnp.swapaxes(ctx_vgrad, 0, 1)
    d_queries = query_sum.reshape(length, responses, HEADS * HEAD_DIM)
    return (d_queries, sys_kgrad, sys_vgrad, d_ctx_key, d_ctx_value, own_kgrad, own_vgrad)


def solution(mesh):
    return jax.shard_map(
        shards,
        mesh=mesh,
        in_specs=(
            P("level", "req", None),
            P("level", "req", None),
            P("level", "req", None),
            P("level", "req", None),
            P("level", None),
            P("level", None),
            P("req", "level", None),
            P("req", "level", None),
            P("req"),
            P("req"),
            P("req"),
        ),
        out_specs=(
            P("level", "req", None),
            P(("level", "req"), None),
            P(("level", "req"), None),
            P("req", "level", None),
            P("req", "level", None),
            P("level", "req", None),
            P("level", "req", None),
        ),
        check_vma=False,
    )
```

profile of v0, /device:TPU:0, one launch (start us, length us, event | category | flops | bytes accessed | tf_op | source)
XLA Modules:
  0.0 329.8 jit_solution(2340916587254903458)
XLA Ops:
  9.4 9.7 %all_gather.19 = bf16[2,128,128]{2,0,1:T(2,128)(2,1)S(1)} all-gather(bf16[2,32,128]{2,0,1:T(2,128)(2,1)S(1)} %copy.89), channel_id=1, replica_groups=mesh['level'=4,'req'=8] {'level'}, dimensions={1}, use_global_device_ids=true | all-gather | bytes 81920 | tf_op jit(solution)/shard_map/all_gather | solution.py:133
  19.4 8.1 %all_gather.18 = bf16[128,128]{1,0:T(8,128)(2,1)S(1)} all-gather(bf16[32,128]{1,0:T(8,128)(2,1)} %param.19), channel_id=1, replica_groups=mesh['level'=4,'req'=8] {'level'}, dimensions={0}, use_global_device_ids=true | all-gather | bytes 40960 | tf_op jit(solution)/shard_map/all_gather | solution.py:131
  28.3 7.4 %all_gather.21 = bf16[2,128,128]{2,0,1:T(2,128)(2,1)S(1)} all-gather(bf16[2,32,128]{2,0,1:T(2,128)(2,1)S(1)} %copy.93), channel_id=1, replica_groups=mesh['level'=4,'req'=8] {'level'}, dimensions={1}, use_global_device_ids=true | all-gather | bytes 81920 | tf_op jit(solution)/shard_map/all_gather | solution.py:134
  36.0 8.0 %all_gather.20 = bf16[128,128]{1,0:T(8,128)(2,1)S(1)} all-gather(bf16[32,128]{1,0:T(8,128)(2,1)} %param.20), channel_id=1, replica_groups=mesh['level'=4,'req'=8] {'level'}, dimensions={0}, use_global_device_ids=true | all-gather | bytes 40960 | tf_op jit(solution)/shard_map/all_gather | solution.py:132
  44.8 1.4 bitcast_select_fusion.3
  47.4 9.2 %all_gather.23 = bf16[256,8,128]{2,0,1:T(8,128)(2,1)S(1)} all-gather(bf16[64,8,128]{2,0,1:T(8,128)(2,1)S(1)} %copy.97), channel_id=1, replica_groups=mesh['level'=4,'req'=8] {'level'}, dimensions={0}, use_global_device_ids=true | all-gather | bytes 655360 | tf_op jit(solution)/shard_map/all_gather | solution.py:136
  56.7 9.9 %all_gather.22 = bf16[256,8,128]{2,0,1:T(8,128)(2,1)S(1)} all-gather(bf16[64,8,128]{2,0,1:T(8,128)(2,1)S(1)} %copy.96), channel_id=1, replica_groups=mesh['level'=4,'req'=8] {'level'}, dimensions={0}, use_global_device_ids=true | all-gather | bytes 655360 | tf_op jit(solution)/shard_map/all_gather | solution.py:135
  66.6 2.0 fusion.41
  70.5 2.1 fusion.35
  72.6 2.1 fusion.38
  74.8 10.2 %while.6 = (s32[]{:T(128)}, f32[8,7,64]{2,1,0:T(8,128)S(1)}, f32[8,7,64]{2,1,0:T(8,128)S(1)}, f32[8,7,64]{2,1,0:T(8,128)S(1)}, s32[2]{0:T(128)S(1)}, /*index=5*/...) while((s32[]{:T(128)}, f32[8,7,64]{2,1,0:T(8,128)S(1)}, ...), condition=%wide.region_11.12_spmd.clone, body=%wide.region_7.11_spmd.clone.sunk | while | flops 240470976 | bytes 8421261 | solution.py:57
  78.6 1.2 fusion.138
  83.7 1.2 fusion.138
  85.1 4.8 %fusion.51 = (bf16[8,128,7,64]{1,3,2,0:T(8,128)(2,1)S(1)}, bf16[8,128,7,64]{1,3,2,0:T(8,128)(2,1)S(1)}, bf16[8,128,7,64]{1,3,2,0:T(8,128)(2,1)}) fusion(f32[8,64,7,128]{3,1,2,0:T(8,128)} %copy-done.10, f32[8,7,64]{2,1,0:T(8,128)S(1)} %get-tuple-element.646, pred[128]{0:T(512)(128)(4,1)S(1)} %iota_compare_fusion.6, f32[8,7,64]{2,1,0:T(8,128)S(1)} %get-tuple-element.649, ...), kind=kLoop, calls=%fused_computation.82 | loop fusion | flops 5963776 | bytes 10122368 | tf_op jit(solution)/shard_map/while/body/eval_jaxpr/convert_element_type | solution.py:99
  92.7 3.1 convolution_bitcast_fusion.2
  95.8 1.3 convolution_bitcast_fusion.4
  97.7 1.3 convolution_bitcast_fusion.5
  99.1 1.6 fusion.78
  100.7 1.6 bitcast_add_fusion.1
  102.4 18.1 %while.7 = (s32[]{:T(128)}, f32[64,8,7,128]{3,0,2,1:T(8,128)}, f32[2,8,128,128]{3,2,1,0:T(8,128)}, f32[2,8,128,128]{3,2,1,0:T(8,128)}, bf16[2,8,128,128]{3,2,1,0...) while((s32[]{:T(128)}, f32[64,8,7,128]{3,0,2,1:T(8,128)}, ...), condition=%wide.region_13.14_spmd.clone, body=%wide.region_12.13_spmd.clone.sunk | while | flops 591536576 | bytes 44386836 | solution.py:103
  106.2 1.1 copy-done
  110.1 1.3 fusion.154
  115.2 1.1 copy-done
  119.1 1.3 fusion.154
  120.4 2.8 copy.116
  123.4 3.0 copy.117
  127.6 2.3 copy.181
  129.9 85.7 %all-reduce.9.cloned.1.call-done = (f32[128,128]{1,0:T(8,128)}, f32[128,128]{1,0:T(8,128)}) async-done(((f32[128,128]{1,0:T(8,128)}, f32[128,128]{1,0:T(8,128)}), (f32[128,128]{1,0:T(8,128)}, f32[128,128]{1,0:T(8,128)})) %all-reduce.9.cloned.1.call-update) | async-done | bytes 131088
  215.7 1.3 constant_dynamic-slice_fusion
  216.9 43.7 %all-reduce.11.cloned.1.call-done = (f32[128,2,128]{2,1,0:T(2,128)}, f32[128,2,128]{2,1,0:T(2,128)}) async-done(((f32[128,2,128]{2,1,0:T(2,128)}, f32[128,2,128]{2,1,0:T(2,128)}), (f32[128,2,128]{2,1,0:T(2,128)}, f32[128,2,128]{2,1,0:T(2,128)})) %all-reduce.11.cloned.1.call-update) | async-done | bytes 262160
  262.7 29.5 %reduce-scatter.3.cloned.1.call-done = f32[64,8,128]{2,1,0:T(8,128)} async-done(((f32[256,8,128]{2,1,0:T(8,128)}), f32[64,8,128]{2,1,0:T(8,128)}) %reduce-scatter.3.cloned.1.call-update) | async-done | bytes 262160 | tf_op jit(solution)/shard_map/reduce_scatter | solution.py:205
  292.2 31.1 %reduce-scatter.5.cloned.1.call-done = f32[64,8,128]{2,1,0:T(8,128)} async-done(((f32[256,8,128]{2,1,0:T(8,128)}), f32[64,8,128]{2,1,0:T(8,128)}) %reduce-scatter.5.cloned.1.call-update) | async-done | bytes 262160 | tf_op jit(solution)/shard_map/reduce_scatter | solution.py:206
  (132 shorter events, 34.2 us)
Async XLA Ops:
  7.2 208.5 %all-reduce.9.cloned.1.call-start = ((), (), s32[]{:S(2)}) async-start(), calls=%async_computation.4 | async-start | bytes 262144
  27.6 41.1 %copy-start.17 = (bf16[128,128]{1,0:T(8,128)(2,1)}, bf16[128,128]{1,0:T(8,128)(2,1)S(1)}, u32[]{:S(2)}) copy-start(bf16[128,128]{1,0:T(8,128)(2,1)S(1)} %all_gather.18) | copy-start | bytes 98308
  44.7 2.4 copy-start.13
  46.2 0.9 copy-start.3
  46.2 1.2 copy-start.19
  47.1 9.5 %copy-start.20 = (bf16[64,8,128]{2,1,0:T(8,128)(2,1)S(1)}, bf16[64,8,128]{2,1,0:T(8,128)(2,1)}, u32[]{:S(2)}) copy-start(bf16[64,8,128]{2,1,0:T(8,128)(2,1)} %param.17) | copy-start | bytes 393220
  66.6 2.0 copy-start.14
  68.6 4.0 %copy-start.9 = (f32[8,128,64,7]{1,2,3,0:T(8,128)}, f32[8,128,64,7]{1,2,3,0:T(8,128)S(1)}, u32[]{:S(2)}) copy-start(f32[8,128,64,7]{1,2,3,0:T(8,128)S(1)} %get-tuple-element.457) | copy-start | bytes 5505028
  68.6 1.8 copy-start.4
  69.4 3.3 copy-start.10
  85.1 4.8 %copy-start.5 = (bf16[64,8,7,128]{3,1,2,0:T(8,128)(2,1)S(1)}, bf16[64,8,7,128]{3,1,2,0:T(8,128)(2,1)}, u32[]{:S(2)}) copy-start(bf16[64,8,7,128]{3,1,2,0:T(8,128)(2,1)} %copy-done.3) | copy-start | bytes 2752516
  89.9 1.1 copy-start.7
  89.9 1.5 copy-start.15
  92.5 168.2 %all-reduce.11.cloned.1.call-start = ((), (), s32[]{:S(2)}) async-start(), calls=%async_computation.5 | async-start | bytes 524288
  92.7 4.4 %copy-start.6 = (bf16[8,128,7,64]{1,3,2,0:T(8,128)(2,1)S(1)}, bf16[8,128,7,64]{1,3,2,0:T(8,128)(2,1)}, u32[]{:S(2)}) copy-start(bf16[8,128,7,64]{1,3,2,0:T(8,128)(2,1)} %get-tuple-element.447) | copy-start | bytes 2752516
  92.7 4.4 %copy-start.16 = (bf16[64,8,896]{2,1,0:T(8,128)(2,1)S(1)}, bf16[64,8,896]{2,1,0:T(8,128)(2,1)}, u32[]{:S(2)}) copy-start(bf16[64,8,896]{2,1,0:T(8,128)(2,1)} %param.15) | copy-start | bytes 2752516
  97.7 3.1 copy-start.18
  99.0 193.2 %reduce-scatter.3.cloned.1.call-start = ((), (), s32[]{:S(2)}) async-start(), calls=%async_computation.2 | async-start | bytes 1310720 | tf_op jit(solution)/shard_map/reduce_scatter | solution.py:205
  99.1 1.7 copy-start.8
  105.8 1.5 copy-start
  107.3 1.2 copy-start.11
  107.8 1.2 copy-start.1
  109.1 1.0 copy-start.12
  114.8 1.5 copy-start
  116.3 1.2 copy-start.11
  116.9 1.2 copy-start.1
  118.1 1.0 copy-start.12
  123.3 3.1 copy-start.21
  123.3 4.3 %copy-start.2 = (f32[64,8,7,128]{3,0,2,1:T(8,128)S(1)}, f32[64,8,7,128]{3,0,2,1:T(8,128)}, u32[]{:S(2)}) copy-start(f32[64,8,7,128]{3,0,2,1:T(8,128)} %get-tuple-element.242) | copy-start | bytes 5505028
  123.3 199.9 %reduce-scatter.5.cloned.1.call-start = ((), (), s32[]{:S(2)}) async-start(), calls=%async_computation.3 | async-start | bytes 1310720 | tf_op jit(solution)/shard_map/reduce_scatter | solution.py:206
Sparse Core Ops, SparseCore 0:
  92.6 123.0 all-reduce.8
  218.6 42.0 all-reduce.10
  264.4 27.7 reduce-scatter.2
  295.5 27.7 reduce-scatter.4
where the time goes:
time: 331 us; the launch traced here: 330 us
  waiting for transfers between devices  190 us (57%)
  blocking collectives  52.3 us (16%)
  matrix products  30.3 us (9%)
  local copies, waits for them, and re-layouts  24.3 us (7%)
  other arithmetic  17.2 us (5%)
  between operations  14.8 us (4%)
    unnamed x6, waiting for transfers between devices  130 us
    reduce_scatter x1, waiting for transfers between devices, shards(): lax.psum_scatter(own_vpart, 'level', scatter_dimension=0, tiled=True)  31.1 us
    reduce_scatter x1, waiting for transfers between devices, shards(): lax.psum_scatter(own_kpart, 'level', scatter_dimension=0, tiled=True)  29.5 us
    all_gather x1, blocking collectives, shards(): lax.all_gather(resp_key, 'level', axis=0, tiled=True)  9.87 us
    all_gather x1, blocking collectives, shards(): lax.all_gather(ctx_key, 'level', axis=1, tiled=True)  9.69 us
    all_gather x1, blocking collectives, shards(): lax.all_gather(resp_value, 'level', axis=0, tiled=True)  9.23 us
    all_gather x1, blocking collectives, shards(): lax.all_gather(sys_key, 'level', axis=0, tiled=True)  8.14 us
    all_gather x1, blocking collectives, shards(): lax.all_gather(sys_value, 'level', axis=0, tiled=True)  8.01 us
  transfers between devices with their start and end apart: 4, of which 4 were waited for; matrix products, arithmetic and copies ran while one was open for 10% of the time, Pallas kernels for 0%

commit v1 on v0

v1 whole, which is shorter than its diff:
```python
import functools
import math

import jax
import jax.numpy as jnp
from jax import lax
from jax.experimental import pallas as pl
from jax.experimental.pallas import tpu as pltpu
from jax.sharding import PartitionSpec as P

HEADS = 7
D = 128
NEGATIVE = -1e30
SCALING = D ** (-0.5)
SCALING2 = SCALING * math.log2(math.e)
F32 = jnp.float32
BF16 = jnp.bfloat16
MESH = pl.DeviceIdType.MESH


def nt(a, b):
    return lax.dot_general(a, b, (((1,), (1,)), ((), ())), preferred_element_type=F32)


def tn(a, b):
    return lax.dot_general(a, b, (((0,), (0,)), ((), ())), preferred_element_type=F32)


def nn(a, b):
    return jnp.dot(a, b, preferred_element_type=F32)


def kernel(
    levels, reqs, T, R, SYS, CTX, C, M,
    q_ref, g_ref, rk_ref, rv_ref, sk_ref, sv_ref, ck_ref, cv_ref, parent, rlen, clen,
    dq_ref, dsk_ref, dsv_ref, dck_ref, dcv_ref, drk_ref, drv_ref,
    qf, gf, kvf, kv, shared, ctx_s, q_s, g_s, s_s, p_s, own_part, own_grad, gsend, grecv,
    shared_acc_sys, shared_acc_ctx, csend, crecv, tsend, trecv,
    kv_ss, kv_rs, sh_ss, sh_rs, gr_ss, gr_rs, cs_ss, cs_rs, t_ss, t_rs,
):
    me = lax.axis_index("level")
    mq = lax.axis_index("req")
    SL, CL = SYS // levels, CTX // levels
    K0, V0 = 0, SL + C * CL
    OWN = levels * T

    barrier = pltpu.get_barrier_semaphore()
    for b in range(levels):
        @pl.when(b != me)
        def _(b=b):
            pl.semaphore_signal(barrier, inc=1, device_id=(b, mq), device_id_type=MESH)
    for b in range(reqs):
        @pl.when(b != mq)
        def _(b=b):
            pl.semaphore_signal(barrier, inc=1, device_id=(me, b), device_id_type=MESH)

    mine = pl.ds(pl.multiple_of(me * T, T), T)
    shared[me, K0:K0 + SL] = sk_ref[...]
    shared[me, V0:V0 + SL] = sv_ref[...]
    for c in range(C):
        shared[me, K0 + SL + c * CL:K0 + SL + (c + 1) * CL] = ck_ref[c]
        shared[me, V0 + SL + c * CL:V0 + SL + (c + 1) * CL] = cv_ref[c]
    kvf[0] = rk_ref[...].astype(F32).reshape(T * R, D)
    kvf[1] = rv_ref[...].astype(F32).reshape(T * R, D)
    for r in range(R):
        for i in range(2):
            kv[r, i, mine, :] = kvf[i, pl.ds(r, T, stride=R), :].astype(BF16)
    for b in range(levels):
        @pl.when(b > me)
        def _(b=b):
            kv[:, :, b * T:(b + 1) * T, :] = jnp.zeros((R, 2, T, D), BF16)

    pl.semaphore_wait(barrier, levels + reqs - 2)

    def shared_copy(dst, src):
        return pltpu.make_async_remote_copy(
            src_ref=shared.at[me], dst_ref=shared.at[me],
            send_sem=sh_ss.at[dst], recv_sem=sh_rs.at[src],
            device_id=(dst, mq), device_id_type=MESH)

    def kv_copy(r, dst, src):
        return pltpu.make_async_remote_copy(
            src_ref=kv.at[r, :, mine, :], dst_ref=kv.at[r, :, mine, :],
            send_sem=kv_ss.at[r, dst], recv_sem=kv_rs.at[r, src],
            device_id=(dst, mq), device_id_type=MESH)

    def grad_copy(r, dst, src):
        return pltpu.make_async_remote_copy(
            src_ref=gsend.at[r, dst], dst_ref=grecv.at[r, src],
            send_sem=gr_ss.at[r, dst], recv_sem=gr_rs.at[r, src],
            device_id=(dst, mq), device_id_type=MESH)

    def sum_copy(dst, src):
        return pltpu.make_async_remote_copy(
            src_ref=csend.at[dst], dst_ref=crecv.at[src],
            send_sem=cs_ss.at[dst], recv_sem=cs_rs.at[src],
            device_id=(dst, mq), device_id_type=MESH)

    def total_copy(dst, src):
        return pltpu.make_async_remote_copy(
            src_ref=tsend.at[dst], dst_ref=trecv.at[src],
            send_sem=t_ss.at[dst], recv_sem=t_rs.at[src],
            device_id=(me, dst), device_id_type=MESH)

    for b in range(levels):
        @pl.when(b != me)
        def _(b=b):
            shared_copy(b, me).start()

    def send_keys(r, carry):
        for b in range(levels):
            @pl.when(b > me)
            def _(b=b):
                kv_copy(r, b, me).start()
        return carry

    lax.fori_loop(0, R, send_keys, 0)

    for h in range(HEADS):
        qf[h] = q_ref[:, :, h * D:(h + 1) * D].astype(F32).reshape(T * R, D)
        gf[h] = g_ref[:, :, h * D:(h + 1) * D].astype(F32).reshape(T * R, D)
    row_at = me * T + lax.broadcasted_iota(jnp.int32, (T, D), 0)

    def arrange(r, carry):
        live = row_at < rlen[r]
        rows = pl.ds(r, T, stride=R)
        for h in range(HEADS):
            q_s[r, h * T:(h + 1) * T, :] = qf[h, rows, :].astype(BF16)
            g_s[r, h * T:(h + 1) * T, :] = jnp.where(live, gf[h, rows, :], 0.0).astype(BF16)
        if M > HEADS * T:
            q_s[r, HEADS * T:, :] = jnp.zeros((M - HEADS * T, D), BF16)
            g_s[r, HEADS * T:, :] = jnp.zeros((M - HEADS * T, D), BF16)
        return carry

    lax.fori_loop(0, R, arrange, 0)
    shared_acc_sys[...] = jnp.zeros(shared_acc_sys.shape, F32)
    shared_acc_ctx[...] = jnp.zeros(shared_acc_ctx.shape, F32)
    crecv[me] = jnp.zeros(crecv.shape[1:], BF16)

    for b in range(levels):
        @pl.when(b != me)
        def _(b=b):
            shared_copy(b, b).wait_recv()

    sgroup = min(levels, max(1, 128 // SL))
    cgroup = min(levels, max(1, 128 // CL))
    own_width = min(128, OWN)
    chunks = []
    at = 0
    for b in range(0, levels, sgroup):
        chunks.append(("sys", b, sgroup * SL, at))
        at += sgroup * SL
    for b in range(0, levels, cgroup):
        chunks.append(("ctx", b, cgroup * CL, at))
        at += cgroup * CL
    for b in range(0, OWN, own_width):
        chunks.append(("own", b, own_width, at))
        at += own_width
    row_of_lane = me * T + lax.rem(lax.broadcasted_iota(jnp.int32, (1, M), 1), T)

    def one_response(r, carry):
        for b in range(levels):
            @pl.when(b < me)
            def _(b=b):
                kv_copy(r, b, b).wait_recv()
        where_ctx = parent[r] - mq * C
        limit = jnp.int32(0)
        chosen = []
        for c in range(C):
            chosen.append(jnp.where(where_ctx == c, 1.0, 0.0))
            limit = limit + jnp.where(where_ctx == c, clen[c], 0)
        for which, base in ((0, K0), (1, V0)):
            picked = jnp.zeros((levels, CL, D), F32)
            for c in range(C):
                at = base + SL + c * CL
                picked = picked + chosen[c] * shared[:, at:at + CL, :].astype(F32)
            ctx_s[which] = picked.astype(BF16).reshape(CTX, D)
        q = q_s[r]
        g = g_s[r]

        def rows_of(kind, start, width, which):
            base = (K0, V0)[which]
            if kind == "sys":
                return shared[start:start + sgroup, base:base + SL, :].reshape(width, D)
            if kind == "ctx":
                return ctx_s[which, start * CL:start * CL + width, :]
            return kv[r, which, start:start + width, :]

        tops = jnp.full((8, M), NEGATIVE, F32)
        for kind, start, width, at in chunks:
            scores = nt(rows_of(kind, start, width, 0), q) * SCALING2
            places = lax.broadcasted_iota(jnp.int32, (width, M), 0)
            if kind == "ctx":
                scores = jnp.where(places + start * CL < limit, scores, NEGATIVE)
            if kind == "own":
                scores = jnp.where(places + start <= row_of_lane, scores, NEGATIVE)
            s_s[at:at + width, :] = scores
            tops = jnp.maximum(tops, jnp.max(scores.reshape(width // 8, 8, M), axis=0))
        top = jnp.max(tops, axis=0, keepdims=True)
        totals = jnp.zeros((8, M), F32)
        running = jnp.zeros((8, M), F32)
        for kind, start, width, at in chunks:
            weights = jnp.exp2(s_s[at:at + width, :] - top)
            products = nt(rows_of(kind, start, width, 1), g)
            s_s[at:at + width, :] = weights
            p_s[at:at + width, :] = products
            totals = totals + jnp.sum(weights.reshape(width // 8, 8, M), axis=0)
            running = running + jnp.sum((weights * products).reshape(width // 8, 8, M), axis=0)
        inverse = 1.0 / jnp.sum(totals, axis=0, keepdims=True)
        deltas = jnp.sum(running, axis=0, keepdims=True) * inverse
        dq = jnp.zeros((D, M), F32)
        for kind, start, width, at in chunks:
            chances = s_s[at:at + width, :] * inverse
            slopes = (chances * (p_s[at:at + width, :] - deltas)).astype(BF16)
            dk = nn(slopes, q) * SCALING
            dv = nn(chances.astype(BF16), g)
            dq = dq + tn(rows_of(kind, start, width, 0), slopes)
            if kind == "sys":
                place = slice(start * SL, start * SL + width)
                shared_acc_sys[0, place] += dk
                shared_acc_sys[1, place] += dv
            if kind == "ctx":
                place = slice(start * CL, start * CL + width)
                for c in range(C):
                    shared_acc_ctx[0, c, place] += dk * chosen[c]
                    shared_acc_ctx[1, c, place] += dv * chosen[c]
            if kind == "own":
                own_part[0, start:start + width] = dk
                own_part[1, start:start + width] = dv
        own_grad[r] = own_part[:, mine, :]
        for b in range(levels):
            @pl.when(b < me)
            def _(b=b):
                gsend[r, b] = own_part[:, b * T:(b + 1) * T, :].astype(BF16)
                grad_copy(r, b, me).start()
        dq_rows = jnp.transpose(dq) * SCALING
        for h in range(HEADS):
            qf[h, pl.ds(r, T, stride=R), :] = dq_rows[h * T:(h + 1) * T]
        return carry

    lax.fori_loop(0, R, one_response, 0)

    for b in range(levels):
        @pl.when(b != me)
        def _(b=b):
            for which, base in ((0, K0), (1, V0)):
                csend[b, base:base + SL] = shared_acc_sys[which, b * SL:(b + 1) * SL].astype(BF16)
                for c in range(C):
                    at = base + SL + c * CL
                    csend[b, at:at + CL] = shared_acc_ctx[which, c, b * CL:(b + 1) * CL].astype(BF16)
            sum_copy(b, me).start()

    for h in range(HEADS):
        dq_ref[:, h * D:(h + 1) * D] = qf[h]

    def finish(r, carry):
        for b in range(levels):
            @pl.when(b > me)
            def _(b=b):
                grad_copy(r, b, b).wait_recv()
                own_grad[r] += grecv[r, b].astype(F32)
        rows = pl.ds(r, T, stride=R)
        drk_ref[rows, :] = own_grad[r, 0]
        drv_ref[rows, :] = own_grad[r, 1]
        return carry

    lax.fori_loop(0, R - 1, finish, 0)

    for b in range(levels):
        @pl.when(b != me)
        def _(b=b):
            sum_copy(b, b).wait_recv()
    rq = SL // reqs
    sys_rows = pl.ds(pl.multiple_of(me * SL, SL), SL)
    ctx_rows = pl.ds(pl.multiple_of(me * CL, CL), CL)
    for which, base in ((0, K0), (1, V0)):
        total = shared_acc_sys[which, sys_rows, :]
        for b in range(levels):
            total = total + crecv[b, base:base + SL, :].astype(F32)
        for b in range(reqs):
            tsend[b, which * rq:(which + 1) * rq, :] = total[b * rq:(b + 1) * rq]
    for b in range(reqs):
        @pl.when(b != mq)
        def _(b=b):
            total_copy(b, mq).start()
    trecv[mq] = tsend[mq]
    for which, base, out in ((0, K0, dck_ref), (1, V0, dcv_ref)):
        for c in range(C):
            at = base + SL + c * CL
            total = shared_acc_ctx[which, c, ctx_rows, :]
            for b in range(levels):
                total = total + crecv[b, at:at + CL, :].astype(F32)
            out[c] = total
    finish(R - 1, 0)

    for b in range(levels):
        @pl.when(b != me)
        def _(b=b):
            shared_copy(b, me).wait_send()
            sum_copy(b, me).wait_send()

    def sent(r, carry):
        for b in range(levels):
            @pl.when(b > me)
            def _(b=b):
                kv_copy(r, b, me).wait_send()

            @pl.when(b < me)
            def _(b=b):
                grad_copy(r, b, me).wait_send()
        return carry

    lax.fori_loop(0, R, sent, 0)
    for b in range(reqs):
        @pl.when(b != mq)
        def _(b=b):
            total_copy(b, mq).wait_send()
            total_copy(b, b).wait_recv()
    grand = trecv[0]
    for b in range(1, reqs):
        grand = grand + trecv[b]
    dsk_ref[...] = grand[:rq]
    dsv_ref[...] = grand[rq:]


def shards(levels, reqs, queries, out_grad, resp_key, resp_value, sys_key, sys_value,
           ctx_key, ctx_value, parent, resp_len, ctx_len):
    T, R, _ = queries.shape
    SL, CL, C = sys_key.shape[0], ctx_key.shape[1], ctx_key.shape[0]
    SYS, CTX = SL * levels, CL * levels
    M = -(-HEADS * T // 128) * 128
    OWN = levels * T
    N = SYS + CTX + OWN
    SH = 2 * (SL + C * CL)
    rq = SL // reqs
    vmem = pl.BlockSpec(memory_space=pltpu.VMEM)
    smem = pl.BlockSpec(memory_space=pltpu.SMEM)
    dma = pltpu.SemaphoreType.DMA
    V = pltpu.VMEM
    outs = pl.pallas_call(
        functools.partial(kernel, levels, reqs, T, R, SYS, CTX, C, M),
        out_shape=(
            jax.ShapeDtypeStruct((T * R, HEADS * D), F32),
            jax.ShapeDtypeStruct((rq, D), F32),
            jax.ShapeDtypeStruct((rq, D), F32),
            jax.ShapeDtypeStruct((C, CL, D), F32),
            jax.ShapeDtypeStruct((C, CL, D), F32),
            jax.ShapeDtypeStruct((T * R, D), F32),
            jax.ShapeDtypeStruct((T * R, D), F32),
        ),
        in_specs=[vmem] * 8 + [smem] * 3,
        out_specs=(vmem,) * 7,
        scratch_shapes=[
            V((HEADS, T * R, D), F32),
            V((HEADS, T * R, D), F32),
            V((2, T * R, D), F32),
            V((R, 2, OWN, D), BF16),
            V((levels, SH, D), BF16),
            V((2, CTX, D), BF16),
            V((R, M, D), BF16),
            V((R, M, D), BF16),
            V((N, M), F32),
            V((N, M), F32),
            V((2, OWN, D), F32),
            V((R, 2, T, D), F32),
            V((R, levels, 2, T, D), BF16),
            V((R, levels, 2, T, D), BF16),
            V((2, SYS, D), F32),
            V((2, C, CTX, D), F32),
            V((levels, SH, D), BF16),
            V((levels, SH, D), BF16),
            V((reqs, 2 * rq, D), F32),
            V((reqs, 2 * rq, D), F32),
            dma((R, levels)), dma((R, levels)),
            dma((levels,)), dma((levels,)),
            dma((R, levels)), dma((R, levels)),
            dma((levels,)), dma((levels,)),
            dma((reqs,)), dma((reqs,)),
        ],
        compiler_params=pltpu.CompilerParams(
            collective_id=0, has_side_effects=True, vmem_limit_bytes=48 * 2**20
        ),
        cost_estimate=pl.CostEstimate(
            flops=10 * R * M * N * D, bytes_accessed=10 * T * R * HEADS * D,
            transcendentals=R * M * N,
        ),
    )(queries, out_grad, resp_key, resp_value, sys_key, sys_value, ctx_key, ctx_value,
      parent, resp_len, ctx_len)
    dq, dsk, dsv, dck, dcv, drk, drv = outs
    return (dq.reshape(T, R, HEADS * D), dsk, dsv, dck, dcv,
            drk.reshape(T, R, D), drv.reshape(T, R, D))


def solution(mesh):
    return jax.shard_map(
        functools.partial(shards, mesh.shape["level"], mesh.shape["req"]),
        mesh=mesh,
        in_specs=(
            P("level", "req", None),
            P("level", "req", None),
            P("level", "req", None),
            P("level", "req", None),
            P("level", None),
            P("level", None),
            P("req", "level", None),
            P("req", "level", None),
            P("req"),
            P("req"),
            P("req"),
        ),
        out_specs=(
            P("level", "req", None),
            P(("level", "req"), None),
            P(("level", "req"), None),
            P("req", "level", None),
            P("req", "level", None),
            P("level", "req", None),
            P("level", "req", None),
        ),
        check_vma=False,
    )
```

time: 331 us -> 51.1 us (0.15)
  waiting for transfers between devices: 190 us -> 0 us
  blocking collectives: 52.3 us -> 0 us
  Pallas kernels: 0 us -> 35.9 us
  matrix products: 30.3 us -> 0 us
  other arithmetic: 17.2 us -> 0 us
  between operations: 14.8 us -> 0.67 us
  local copies, waits for them, and re-layouts: 24.3 us -> 14 us
    unnamed x6 -> x0, waiting for transfers between devices: 130 us -> none
    reduce_scatter x2 -> x0, waiting for transfers between devices: 60.6 us -> none  [the longest x1 31.1 us: shards(): lax.psum_scatter(own_vpart, 'level', scatter_dimension=0, tiled=True)]
    all_gather x6 -> x0, blocking collectives: 52.3 us -> none  [the longest x1 9.87 us: shards(): lax.all_gather(resp_key, 'level', axis=0, tiled=True)]
    pallas_call x0 -> x1, Pallas kernels: none -> 35.9 us  [shards(): pl.pallas_call(functools.partial(kernel, levels, reqs, T, R, SYS, CTX, C,...]
    dot_general x25 -> x0, matrix products: 27.9 us -> none  [the longest x4 6.79 us: backward_advance(): jnp.einsum(grad_form, chances.astype(jnp.bfloat16), grads_all, preferred_...]
    while x19 -> x0, local copies, waits for them, and re-layouts: 7.99 us -> none
    unnamed x46 -> x29, local copies, waits for them, and re-layouts: 6.98 us -> 14 us
    transpose x3 -> x0, local copies, waits for them, and re-layouts: 6.57 us -> none  [the longest x1 2.98 us: backward_segment(): value_grads = jnp.swapaxes(grads_pair[1], 0, 1).reshape(value_rows.shape)]
  transfers between devices with their start and end apart: 4 -> 0, of which waited for: 4 -> 0; matrix products, arithmetic and copies ran while one was open for 10% -> 0% of each run, Pallas kernels for 0% -> 0%
where the time goes in v1:
time: 51.1 us; the launch traced here: 50.6 us
  Pallas kernels  35.9 us (70%)
  local copies, waits for them, and re-layouts  14 us (27%)
  between operations  0.67 us (1%)
    pallas_call x1, Pallas kernels, shards(): pl.pallas_call(functools.partial(kernel, levels, reqs, T, R, SYS, CTX, C,...  35.9 us
    unnamed x29, local copies, waits for them, and re-layouts  14 us

profile of v1, /device:TPU:0, one launch (start us, length us, event | category | flops | bytes accessed | tf_op | source)
XLA Modules:
  0.0 50.6 jit_solution(6689694369584011770)
XLA Ops:
  0.6 0.0 copy-start
  0.6 1.2 %copy-done = bf16[64,8,896]{2,1,0:T(8,128)(2,1)S(1)} copy-done((bf16[64,8,896]{2,1,0:T(8,128)(2,1)S(1)}, bf16[64,8,896]{2,1,0:T(8,128)(2,1)}, u32[]{:S(2)}) %copy-start) | copy-done | bytes 917528
  1.8 0.0 copy-start.1
  1.8 1.2 %copy-done.1 = bf16[64,8,896]{2,1,0:T(8,128)(2,1)S(1)} copy-done((bf16[64,8,896]{2,1,0:T(8,128)(2,1)S(1)}, bf16[64,8,896]{2,1,0:T(8,128)(2,1)}, u32[]{:S(2)}) %copy-start.1) | copy-done | bytes 917528
  3.0 0.0 copy-start.2
  3.0 0.9 %copy-done.2 = bf16[64,8,128]{2,1,0:T(8,128)(2,1)S(1)} copy-done((bf16[64,8,128]{2,1,0:T(8,128)(2,1)S(1)}, bf16[64,8,128]{2,1,0:T(8,128)(2,1)}, u32[]{:S(2)}) %copy-start.2) | copy-done | bytes 131096
  3.9 0.0 copy-start.3
  3.9 0.9 %copy-done.3 = bf16[64,8,128]{2,1,0:T(8,128)(2,1)S(1)} copy-done((bf16[64,8,128]{2,1,0:T(8,128)(2,1)S(1)}, bf16[64,8,128]{2,1,0:T(8,128)(2,1)}, u32[]{:S(2)}) %copy-start.3) | copy-done | bytes 131096
  4.8 0.0 copy-start.4
  4.8 0.7 %copy-done.4 = bf16[2,32,128]{2,1,0:T(8,128)(2,1)S(1)} copy-done((bf16[2,32,128]{2,1,0:T(8,128)(2,1)S(1)}, bf16[2,32,128]{2,1,0:T(8,128)(2,1)}, u32[]{:S(2)}) %copy-start.4) | copy-done | bytes 16408
  5.5 0.0 copy-start.5
  5.5 0.7 %copy-done.5 = bf16[2,32,128]{2,1,0:T(8,128)(2,1)S(1)} copy-done((bf16[2,32,128]{2,1,0:T(8,128)(2,1)S(1)}, bf16[2,32,128]{2,1,0:T(8,128)(2,1)}, u32[]{:S(2)}) %copy-start.5) | copy-done | bytes 16408
  6.2 0.0 copy-start.6
  6.2 0.7 %copy-done.6 = bf16[32,128]{1,0:T(8,128)(2,1)S(1)} copy-done((bf16[32,128]{1,0:T(8,128)(2,1)S(1)}, bf16[32,128]{1,0:T(8,128)(2,1)}, u32[]{:S(2)}) %copy-start.6) | copy-done | bytes 8216
  6.9 0.0 copy-start.7
  6.9 0.7 %copy-done.7 = bf16[32,128]{1,0:T(8,128)(2,1)S(1)} copy-done((bf16[32,128]{1,0:T(8,128)(2,1)S(1)}, bf16[32,128]{1,0:T(8,128)(2,1)}, u32[]{:S(2)}) %copy-start.7) | copy-done | bytes 8216
  7.6 0.0 copy-start.8
  7.6 0.7 %copy-done.8 = s32[8]{0:T(128)S(1)} copy-done((s32[8]{0:T(128)S(1)}, s32[8]{0:T(128)}, u32[]{:S(2)}) %copy-start.8) | copy-done | bytes 56
  8.3 0.0 copy-start.9
  8.3 0.7 %copy-done.9 = s32[8]{0:T(128)S(1)} copy-done((s32[8]{0:T(128)S(1)}, s32[8]{0:T(128)}, u32[]{:S(2)}) %copy-start.9) | copy-done | bytes 56
  8.9 0.0 copy-start.10
  8.9 0.7 %copy-done.10 = s32[2]{0:T(128)S(1)} copy-done((s32[2]{0:T(128)S(1)}, s32[2]{0:T(128)}, u32[]{:S(2)}) %copy-start.10) | copy-done | bytes 32
  9.6 35.9 %shard_map.162 = (f32[512,896]{1,0:T(8,128)S(1)}, f32[4,128]{1,0:T(4,128)S(1)}, f32[4,128]{1,0:T(4,128)S(1)}, f32[2,32,128]{2,1,0:T(8,128)S(1)}, f32[2,32,128]{2...) custom-call(bf16[64,8,896]{2,1,0:T(8,128)(2,1)S(1)} %copy-done, bf16[64,8,896]{2,1,0:T(8,128)(2,1)S(1)} %copy-done.1, ...), custom_call_target="tpu_custom_call" | custom-call | flops 2684354560 | bytes 4587520 | tf_op jit(solution)/shard_map/pallas_call | solution.py:340
  45.6 1.2 %copy.25 = f32[64,8,896]{2,1,0:T(8,128)} copy(f32[64,8,896]{2,1,0:T(8,128)S(1)} %bitcast.3) | data formatting | bytes 3670016
  46.8 0.6 %copy.26 = f32[4,128]{1,0:T(4,128)} copy(f32[4,128]{1,0:T(4,128)S(1)} %get-tuple-element.29) | data formatting | bytes 4096
  47.4 0.6 %copy.27 = f32[4,128]{1,0:T(4,128)} copy(f32[4,128]{1,0:T(4,128)S(1)} %get-tuple-element.30) | data formatting | bytes 4096
  47.9 0.6 %copy.28 = f32[2,32,128]{2,1,0:T(8,128)} copy(f32[2,32,128]{2,1,0:T(8,128)S(1)} %get-tuple-element.31) | data formatting | bytes 65536
  48.6 0.6 %copy.29 = f32[2,32,128]{2,1,0:T(8,128)} copy(f32[2,32,128]{2,1,0:T(8,128)S(1)} %get-tuple-element.32) | data formatting | bytes 65536
  49.2 0.7 %copy.30 = f32[64,8,128]{2,1,0:T(8,128)} copy(f32[64,8,128]{2,1,0:T(8,128)S(1)} %bitcast.5) | data formatting | bytes 524288
  49.9 0.7 %copy.31 = f32[64,8,128]{2,1,0:T(8,128)} copy(f32[64,8,128]{2,1,0:T(8,128)S(1)} %bitcast.4) | data formatting | bytes 524288
Async XLA Ops:
  0.6 1.2 %copy-start = (bf16[64,8,896]{2,1,0:T(8,128)(2,1)S(1)}, bf16[64,8,896]{2,1,0:T(8,128)(2,1)}, u32[]{:S(2)}) copy-start(bf16[64,8,896]{2,1,0:T(8,128)(2,1)} %q_ref.1) | copy-start | bytes 2752516
  1.8 1.2 %copy-start.1 = (bf16[64,8,896]{2,1,0:T(8,128)(2,1)S(1)}, bf16[64,8,896]{2,1,0:T(8,128)(2,1)}, u32[]{:S(2)}) copy-start(bf16[64,8,896]{2,1,0:T(8,128)(2,1)} %g_ref.1) | copy-start | bytes 2752516
  3.0 0.9 %copy-start.2 = (bf16[64,8,128]{2,1,0:T(8,128)(2,1)S(1)}, bf16[64,8,128]{2,1,0:T(8,128)(2,1)}, u32[]{:S(2)}) copy-start(bf16[64,8,128]{2,1,0:T(8,128)(2,1)} %rk_ref.1) | copy-start | bytes 393220
  3.9 0.9 %copy-start.3 = (bf16[64,8,128]{2,1,0:T(8,128)(2,1)S(1)}, bf16[64,8,128]{2,1,0:T(8,128)(2,1)}, u32[]{:S(2)}) copy-start(bf16[64,8,128]{2,1,0:T(8,128)(2,1)} %rv_ref.1) | copy-start | bytes 393220
  4.8 0.7 %copy-start.4 = (bf16[2,32,128]{2,1,0:T(8,128)(2,1)S(1)}, bf16[2,32,128]{2,1,0:T(8,128)(2,1)}, u32[]{:S(2)}) copy-start(bf16[2,32,128]{2,1,0:T(8,128)(2,1)} %ck_ref.1) | copy-start | bytes 49156
  5.5 0.7 %copy-start.5 = (bf16[2,32,128]{2,1,0:T(8,128)(2,1)S(1)}, bf16[2,32,128]{2,1,0:T(8,128)(2,1)}, u32[]{:S(2)}) copy-start(bf16[2,32,128]{2,1,0:T(8,128)(2,1)} %cv_ref.1) | copy-start | bytes 49156
  6.2 0.7 %copy-start.6 = (bf16[32,128]{1,0:T(8,128)(2,1)S(1)}, bf16[32,128]{1,0:T(8,128)(2,1)}, u32[]{:S(2)}) copy-start(bf16[32,128]{1,0:T(8,128)(2,1)} %sk_ref.1) | copy-start | bytes 24580
  6.9 0.7 %copy-start.7 = (bf16[32,128]{1,0:T(8,128)(2,1)S(1)}, bf16[32,128]{1,0:T(8,128)(2,1)}, u32[]{:S(2)}) copy-start(bf16[32,128]{1,0:T(8,128)(2,1)} %sv_ref.1) | copy-start | bytes 24580
  7.6 0.7 %copy-start.8 = (s32[8]{0:T(128)S(1)}, s32[8]{0:T(128)}, u32[]{:S(2)}) copy-start(s32[8]{0:T(128)} %parent.1) | copy-start | bytes 100
  8.3 0.7 %copy-start.9 = (s32[8]{0:T(128)S(1)}, s32[8]{0:T(128)}, u32[]{:S(2)}) copy-start(s32[8]{0:T(128)} %rlen.1) | copy-start | bytes 100
  8.9 0.7 %copy-start.10 = (s32[2]{0:T(128)S(1)}, s32[2]{0:T(128)}, u32[]{:S(2)}) copy-start(s32[2]{0:T(128)} %clen.1) | copy-start | bytes 28

commit v2 on v1

--- a/solution.py
+++ b/solution.py
@@ -32,9 +32,9 @@
 
 def kernel(
     levels, reqs, T, R, SYS, CTX, C, M,
-    q_ref, g_ref, rk_ref, rv_ref, sk_ref, sv_ref, ck_ref, cv_ref, parent, rlen, clen,
-    dq_ref, dsk_ref, dsv_ref, dck_ref, dcv_ref, drk_ref, drv_ref,
-    qf, gf, kvf, kv, shared, ctx_s, q_s, g_s, s_s, p_s, own_part, own_grad, gsend, grecv,
+    q_in, g_in, rk_in, rv_in, sk_in, sv_in, ck_in, cv_in, parent_in, rlen_in, clen_in,
+    dq_out, dsk_ref, dsv_ref, dck_ref, dcv_ref, drk_ref, drv_ref,
+    q_ref, g_ref, rk_ref, rv_ref, parent, rlen, clen, in_s, dq_ref, dq_s, qf, gf, kvf, kv, shared, ctx_s, q_s, g_s, s_s, p_s, own_part, own_grad, gsend, grecv,
     shared_acc_sys, shared_acc_ctx, csend, crecv, tsend, trecv,
     kv_ss, kv_rs, sh_ss, sh_rs, gr_ss, gr_rs, cs_ss, cs_rs, t_ss, t_rs,
 ):
@@ -54,12 +54,30 @@
         def _(b=b):
             pl.semaphore_signal(barrier, inc=1, device_id=(me, b), device_id_type=MESH)
 
+    loads = []
+
+    def load(src, dst):
+        copy = pltpu.make_async_copy(src, dst, in_s.at[len(loads)])
+        copy.start()
+        loads.append(copy)
+
+    load(rk_in, rk_ref)
+    load(rv_in, rv_ref)
+    load(sk_in, shared.at[me, K0:K0 + SL])
+    load(sv_in, shared.at[me, V0:V0 + SL])
+    for c in range(C):
+        load(ck_in.at[c], shared.at[me, K0 + SL + c * CL:K0 + SL + (c + 1) * CL])
+        load(cv_in.at[c], shared.at[me, V0 + SL + c * CL:V0 + SL + (c + 1) * CL])
+    first = len(loads)
+    load(q_in, q_ref)
+    load(g_in, g_ref)
+    load(parent_in, parent)
+    load(rlen_in, rlen)
+    load(clen_in, clen)
+
     mine = pl.ds(pl.multiple_of(me * T, T), T)
-    shared[me, K0:K0 + SL] = sk_ref[...]
-    shared[me, V0:V0 + SL] = sv_ref[...]
-    for c in range(C):
-        shared[me, K0 + SL + c * CL:K0 + SL + (c + 1) * CL] = ck_ref[c]
-        shared[me, V0 + SL + c * CL:V0 + SL + (c + 1) * CL] = cv_ref[c]
+    for copy in loads[:2]:
+        copy.wait()
     kvf[0] = rk_ref[...].astype(F32).reshape(T * R, D)
     kvf[1] = rv_ref[...].astype(F32).reshape(T * R, D)
     for r in range(R):
@@ -70,6 +88,8 @@
         def _(b=b):
             kv[:, :, b * T:(b + 1) * T, :] = jnp.zeros((R, 2, T, D), BF16)
 
+    for copy in loads[2:first]:
+        copy.wait()
     pl.semaphore_wait(barrier, levels + reqs - 2)
 
     def shared_copy(dst, src):
@@ -116,6 +136,8 @@
 
     lax.fori_loop(0, R, send_keys, 0)
 
+    for copy in loads[first:]:
+        copy.wait()
     for h in range(HEADS):
         qf[h] = q_ref[:, :, h * D:(h + 1) * D].astype(F32).reshape(T * R, D)
         gf[h] = g_ref[:, :, h * D:(h + 1) * D].astype(F32).reshape(T * R, D)
@@ -235,10 +257,12 @@
                 grad_copy(r, b, me).start()
         dq_rows = jnp.transpose(dq) * SCALING
         for h in range(HEADS):
-            qf[h, pl.ds(r, T, stride=R), :] = dq_rows[h * T:(h + 1) * T]
+            dq_ref[h, pl.ds(r, T, stride=R), :] = dq_rows[h * T:(h + 1) * T]
         return carry
 
     lax.fori_loop(0, R, one_response, 0)
+    dq_copy = pltpu.make_async_copy(dq_ref, dq_out, dq_s)
+    dq_copy.start()
 
     for b in range(levels):
         @pl.when(b != me)
@@ -249,9 +273,6 @@
                     at = base + SL + c * CL
                     csend[b, at:at + CL] = shared_acc_ctx[which, c, b * CL:(b + 1) * CL].astype(BF16)
             sum_copy(b, me).start()
-
-    for h in range(HEADS):
-        dq_ref[:, h * D:(h + 1) * D] = qf[h]
 
     def finish(r, carry):
         for b in range(levels):
@@ -316,11 +337,25 @@
         def _(b=b):
             total_copy(b, mq).wait_send()
             total_copy(b, b).wait_recv()
+    dq_copy.wait()
     grand = trecv[0]
     for b in range(1, reqs):
         grand = grand + trecv[b]
     dsk_ref[...] = grand[:rq]
     dsv_ref[...] = grand[rq:]
+
+
+def write_out(*refs):
+    ins, outs, sems = refs[:7], refs[7:14], refs[14]
+    pairs = [(ins[0].at[h], outs[0].at[:, :, h * D:(h + 1) * D]) for h in range(HEADS)]
+    pairs += list(zip(ins[1:], outs[1:]))
+    copies = [
+        pltpu.make_async_copy(src, dst, sems.at[i]) for i, (src, dst) in enumerate(pairs)
+    ]
+    for copy in copies:
+        copy.start()
+    for copy in copies:
+        copy.wait()
 
 
 def shards(levels, reqs, queries, out_grad, resp_key, resp_value, sys_key, sys_value,
@@ -334,13 +369,13 @@
     SH = 2 * (SL + C * CL)
     rq = SL // reqs
     vmem = pl.BlockSpec(memory_space=pltpu.VMEM)
-    smem = pl.BlockSpec(memory_space=pltpu.SMEM)
+    any_place = pl.BlockSpec(memory_space=pl.ANY)
     dma = pltpu.SemaphoreType.DMA
     V = pltpu.VMEM
     outs = pl.pallas_call(
         functools.partial(kernel, levels, reqs, T, R, SYS, CTX, C, M),
         out_shape=(
-            jax.ShapeDtypeStruct((T * R, HEADS * D), F32),
+            jax.ShapeDtypeStruct((HEADS, T * R, D), F32),
             jax.ShapeDtypeStruct((rq, D), F32),
             jax.ShapeDtypeStruct((rq, D), F32),
             jax.ShapeDtypeStruct((C, CL, D), F32),
@@ -348,9 +383,19 @@
             jax.ShapeDtypeStruct((T * R, D), F32),
             jax.ShapeDtypeStruct((T * R, D), F32),
         ),
-        in_specs=[vmem] * 8 + [smem] * 3,
-        out_specs=(vmem,) * 7,
+        in_specs=[any_place] * 11,
+        out_specs=(any_place,) + (vmem,) * 6,
         scratch_shapes=[
+            V((T, R, HEADS * D), BF16),
+            V((T, R, HEADS * D), BF16),
+            V((T, R, D), BF16),
+            V((T, R, D), BF16),
+            pltpu.SMEM((R,), jnp.int32),
+            pltpu.SMEM((R,), jnp.int32),
+            pltpu.SMEM((C,), jnp.int32),
+            dma((9 + 2 * C,)),
+            V((HEADS, T * R, D), F32),
+            dma(()),
             V((HEADS, T * R, D), F32),
             V((HEADS, T * R, D), F32),
             V((2, T * R, D), F32),
@@ -378,7 +423,7 @@
             dma((reqs,)), dma((reqs,)),
         ],
         compiler_params=pltpu.CompilerParams(
-            collective_id=0, has_side_effects=True, vmem_limit_bytes=48 * 2**20
+            collective_id=0, has_side_effects=True, vmem_limit_bytes=56 * 2**20
         ),
         cost_estimate=pl.CostEstimate(
             flops=10 * R * M * N * D, bytes_accessed=10 * T * R * HEADS * D,
@@ -387,8 +432,17 @@
     )(queries, out_grad, resp_key, resp_value, sys_key, sys_value, ctx_key, ctx_value,
       parent, resp_len, ctx_len)
     dq, dsk, dsv, dck, dcv, drk, drv = outs
-    return (dq.reshape(T, R, HEADS * D), dsk, dsv, dck, dcv,
-            drk.reshape(T, R, D), drv.reshape(T, R, D))
+    finals = (dq.reshape(HEADS, T, R, D), dsk, dsv, dck, dcv,
+              drk.reshape(T, R, D), drv.reshape(T, R, D))
+    shapes = ((T, R, HEADS * D),) + tuple(a.shape for a in finals[1:])
+    return pl.pallas_call(
+        write_out,
+        out_shape=tuple(jax.ShapeDtypeStruct(shape, F32) for shape in shapes),
+        in_specs=[any_place] * 7,
+        out_specs=(any_place,) * 7,
+        scratch_shapes=[dma((HEADS + 6,))],
+        compiler_params=pltpu.CompilerParams(vmem_limit_bytes=56 * 2**20),
+    )(*finals)
 
 
 def solution(mesh):

time: 51.1 us -> 112 us (2.19)
  Pallas kernels: 35.9 us -> 111 us
  local copies, waits for them, and re-layouts: 14 us -> 0 us
    pallas_call x0 -> x1, Pallas kernels: none -> 74.8 us  [shards(): pl.pallas_call(write_out, out_shape=tuple((jax.ShapeDtypeStruct(shape, F3...]
    unnamed x29 -> x0, local copies, waits for them, and re-layouts: 14 us -> none
where the time goes in v2:
time: 112 us
  Pallas kernels  111 us (99%)
    pallas_call x1, Pallas kernels, shards(): pl.pallas_call(write_out, out_shape=tuple((jax.ShapeDtypeStruct(shape, F3...  74.8 us
    pallas_call x1, Pallas kernels, shards(): pl.pallas_call(functools.partial(kernel, levels, reqs, T, R, SYS, CTX, C,...  36.4 us

profile of v2, /device:TPU:0, one launch (start us, length us, event | category | flops | bytes accessed | tf_op | source)
XLA Modules:
  0.0 111.9 jit_solution(12640107207900736776)
XLA Ops:
  0.6 36.4 %shard_map.162 = (f32[7,512,128]{2,1,0:T(8,128)}, f32[4,128]{1,0:T(4,128)}, f32[4,128]{1,0:T(4,128)}, f32[2,32,128]{2,1,0:T(8,128)}, f32[2,32,128]{2,1,0:T(8,128...) custom-call(bf16[64,8,896]{2,1,0:T(8,128)(2,1)} %q_in.1, bf16[64,8,896]{2,1,0:T(8,128)(2,1)} %g_in.1, ...), custom_call_target="tpu_custom_call" | custom-call | flops 2684354560 | bytes 4587520 | tf_op jit(solution)/shard_map/pallas_call | solution.py:375
  37.1 74.8 %shard_map.163 = (f32[64,8,896]{2,1,0:T(8,128)}, f32[4,128]{1,0:T(4,128)}, f32[4,128]{1,0:T(4,128)}, f32[2,32,128]{2,1,0:T(8,128)}, f32[2,32,128]{2,1,0:T(8,128)...) custom-call(f32[7,64,8,128]{3,2,1,0:T(8,128)} %bitcast.3, f32[4,128]{1,0:T(4,128)} %get-tuple-element.15.refs_1_, ...), custom_call_target="tpu_custom_call" | custom-call | tf_op jit(solution)/shard_map/pallas_call | solution.py:438

commit v3 on v2

--- a/solution.py
+++ b/solution.py
@@ -31,10 +31,10 @@
 
 
 def kernel(
-    levels, reqs, T, R, SYS, CTX, C, M,
+    levels, reqs, T, R, SYS, CTX, C, M, PAIR,
     q_in, g_in, rk_in, rv_in, sk_in, sv_in, ck_in, cv_in, parent_in, rlen_in, clen_in,
     dq_out, dsk_ref, dsv_ref, dck_ref, dcv_ref, drk_ref, drv_ref,
-    q_ref, g_ref, rk_ref, rv_ref, parent, rlen, clen, in_s, dq_ref, dq_s, qf, gf, kvf, kv, shared, ctx_s, q_s, g_s, s_s, p_s, own_part, own_grad, gsend, grecv,
+    q_ref, g_ref, rk_ref, rv_ref, parent, rlen, clen, in_s, dq_ref, dq_s, qf, gf, kvf, kv, shared, keys, q_s, g_s, s_s, p_s, ch_s, sl_s, own_part, own_grad, gsend, grecv,
     shared_acc_sys, shared_acc_ctx, csend, crecv, tsend, trecv,
     kv_ss, kv_rs, sh_ss, sh_rs, gr_ss, gr_rs, cs_ss, cs_rs, t_ss, t_rs,
 ):
@@ -164,103 +164,105 @@
         def _(b=b):
             shared_copy(b, b).wait_recv()
 
-    sgroup = min(levels, max(1, 128 // SL))
-    cgroup = min(levels, max(1, 128 // CL))
-    own_width = min(128, OWN)
     chunks = []
-    at = 0
-    for b in range(0, levels, sgroup):
-        chunks.append(("sys", b, sgroup * SL, at))
-        at += sgroup * SL
-    for b in range(0, levels, cgroup):
-        chunks.append(("ctx", b, cgroup * CL, at))
-        at += cgroup * CL
-    for b in range(0, OWN, own_width):
-        chunks.append(("own", b, own_width, at))
-        at += own_width
+    for kind, begin, length in (("sys", 0, SYS), ("ctx", SYS, CTX), ("own", SYS + CTX, OWN)):
+        width = min(128, length)
+        for start in range(0, length, width):
+            chunks.append((kind, start, width, slice(begin + start, begin + start + width)))
     row_of_lane = me * T + lax.rem(lax.broadcasted_iota(jnp.int32, (1, M), 1), T)
-
-    def one_response(r, carry):
-        for b in range(levels):
-            @pl.when(b < me)
-            def _(b=b):
-                kv_copy(r, b, b).wait_recv()
+    for j in range(PAIR):
+        for i, base in ((0, K0), (1, V0)):
+            keys[j, i, :SYS, :] = shared[:, base:base + SL, :].reshape(SYS, D)
+
+    def prepare(j, r):
         where_ctx = parent[r] - mq * C
         limit = jnp.int32(0)
         chosen = []
         for c in range(C):
             chosen.append(jnp.where(where_ctx == c, 1.0, 0.0))
             limit = limit + jnp.where(where_ctx == c, clen[c], 0)
-        for which, base in ((0, K0), (1, V0)):
+        for i, base in ((0, K0), (1, V0)):
             picked = jnp.zeros((levels, CL, D), F32)
             for c in range(C):
                 at = base + SL + c * CL
                 picked = picked + chosen[c] * shared[:, at:at + CL, :].astype(F32)
-            ctx_s[which] = picked.astype(BF16).reshape(CTX, D)
-        q = q_s[r]
-        g = g_s[r]
-
-        def rows_of(kind, start, width, which):
-            base = (K0, V0)[which]
-            if kind == "sys":
-                return shared[start:start + sgroup, base:base + SL, :].reshape(width, D)
-            if kind == "ctx":
-                return ctx_s[which, start * CL:start * CL + width, :]
-            return kv[r, which, start:start + width, :]
-
+            keys[j, i, SYS:SYS + CTX, :] = picked.astype(BF16).reshape(CTX, D)
+            keys[j, i, SYS + CTX:, :] = kv[r, i]
+        s_s[j] = nt(keys[j, 0], q_s[r])
+        p_s[j] = nt(keys[j, 1], g_s[r])
+        return chosen, limit
+
+    def maxima(j, limit):
         tops = jnp.full((8, M), NEGATIVE, F32)
         for kind, start, width, at in chunks:
-            scores = nt(rows_of(kind, start, width, 0), q) * SCALING2
+            scores = s_s[j, at, :] * SCALING2
             places = lax.broadcasted_iota(jnp.int32, (width, M), 0)
             if kind == "ctx":
-                scores = jnp.where(places + start * CL < limit, scores, NEGATIVE)
+                scores = jnp.where(places < limit - start, scores, NEGATIVE)
             if kind == "own":
-                scores = jnp.where(places + start <= row_of_lane, scores, NEGATIVE)
-            s_s[at:at + width, :] = scores
+                scores = jnp.where(places <= row_of_lane - start, scores, NEGATIVE)
+            if kind != "sys":
+                s_s[j, at, :] = scores
             tops = jnp.maximum(tops, jnp.max(scores.reshape(width // 8, 8, M), axis=0))
-        top = jnp.max(tops, axis=0, keepdims=True)
+        return jnp.max(tops, axis=0, keepdims=True)
+
+    def sums(j, top):
         totals = jnp.zeros((8, M), F32)
         running = jnp.zeros((8, M), F32)
         for kind, start, width, at in chunks:
-            weights = jnp.exp2(s_s[at:at + width, :] - top)
-            products = nt(rows_of(kind, start, width, 1), g)
-            s_s[at:at + width, :] = weights
-            p_s[at:at + width, :] = products
+            scores = s_s[j, at, :]
+            if kind == "sys":
+                scores = scores * SCALING2
+            weights = jnp.exp2(scores - top)
+            s_s[j, at, :] = weights
             totals = totals + jnp.sum(weights.reshape(width // 8, 8, M), axis=0)
-            running = running + jnp.sum((weights * products).reshape(width // 8, 8, M), axis=0)
+            parts = weights * p_s[j, at, :]
+            running = running + jnp.sum(parts.reshape(width // 8, 8, M), axis=0)
         inverse = 1.0 / jnp.sum(totals, axis=0, keepdims=True)
-        deltas = jnp.sum(running, axis=0, keepdims=True) * inverse
-        dq = jnp.zeros((D, M), F32)
+        return inverse, jnp.sum(running, axis=0, keepdims=True) * inverse
+
+    def roundings(j, inverse, deltas):
         for kind, start, width, at in chunks:
-            chances = s_s[at:at + width, :] * inverse
-            slopes = (chances * (p_s[at:at + width, :] - deltas)).astype(BF16)
-            dk = nn(slopes, q) * SCALING
-            dv = nn(chances.astype(BF16), g)
-            dq = dq + tn(rows_of(kind, start, width, 0), slopes)
-            if kind == "sys":
-                place = slice(start * SL, start * SL + width)
-                shared_acc_sys[0, place] += dk
-                shared_acc_sys[1, place] += dv
-            if kind == "ctx":
-                place = slice(start * CL, start * CL + width)
-                for c in range(C):
-                    shared_acc_ctx[0, c, place] += dk * chosen[c]
-                    shared_acc_ctx[1, c, place] += dv * chosen[c]
-            if kind == "own":
-                own_part[0, start:start + width] = dk
-                own_part[1, start:start + width] = dv
-        own_grad[r] = own_part[:, mine, :]
-        for b in range(levels):
-            @pl.when(b < me)
-            def _(b=b):
-                gsend[r, b] = own_part[:, b * T:(b + 1) * T, :].astype(BF16)
-                grad_copy(r, b, me).start()
-        dq_rows = jnp.transpose(dq) * SCALING
+            chances = s_s[j, at, :] * inverse
+            ch_s[j, at, :] = chances.astype(BF16)
+            sl_s[j, at, :] = (chances * (p_s[j, at, :] - deltas)).astype(BF16)
+
+    def gradients(j, r, chosen):
+        dk = nn(sl_s[j], q_s[r]) * SCALING
+        dv = nn(ch_s[j], g_s[r])
+        for i, grad in ((0, dk), (1, dv)):
+            shared_acc_sys[i] += grad[:SYS]
+            for c in range(C):
+                shared_acc_ctx[i, c] += grad[SYS:SYS + CTX] * chosen[c]
+            own_part[j, i] = grad[SYS + CTX:]
+        dq_rows = jnp.transpose(tn(keys[j, 0], sl_s[j])) * SCALING
         for h in range(HEADS):
             dq_ref[h, pl.ds(r, T, stride=R), :] = dq_rows[h * T:(h + 1) * T]
+
+    def responses(step, carry):
+        rs = [step * PAIR + j for j in range(PAIR)]
+        for b in range(levels):
+            @pl.when(b < me)
+            def _(b=b):
+                for r in rs:
+                    kv_copy(r, b, b).wait_recv()
+        ready = [prepare(j, r) for j, r in enumerate(rs)]
+        tops = [maxima(j, ready[j][1]) for j in range(PAIR)]
+        for j, r in enumerate(rs):
+            roundings(j, *sums(j, tops[j]))
+        for j, r in enumerate(rs):
+            gradients(j, r, ready[j][0])
+        for j, r in enumerate(rs):
+            own_grad[r] = own_part[j, :, mine, :]
+        for b in range(levels):
+            @pl.when(b < me)
+            def _(b=b):
+                for j, r in enumerate(rs):
+                    gsend[r, b] = own_part[j, :, b * T:(b + 1) * T, :].astype(BF16)
+                    grad_copy(r, b, me).start()
         return carry
 
-    lax.fori_loop(0, R, one_response, 0)
+    lax.fori_loop(0, R // PAIR, responses, 0)
     dq_copy = pltpu.make_async_copy(dq_ref, dq_out, dq_s)
     dq_copy.start()
 
@@ -346,15 +348,20 @@
 
 
 def write_out(*refs):
-    ins, outs, sems = refs[:7], refs[7:14], refs[14]
-    pairs = [(ins[0].at[h], outs[0].at[:, :, h * D:(h + 1) * D]) for h in range(HEADS)]
-    pairs += list(zip(ins[1:], outs[1:]))
-    copies = [
-        pltpu.make_async_copy(src, dst, sems.at[i]) for i, (src, dst) in enumerate(pairs)
-    ]
-    for copy in copies:
+    ins, outs, held, sem_in, sem_out = refs[:7], refs[7:14], refs[14:21], refs[21], refs[22]
+    pieces = [(ins[0].at[h], held[0].at[h], outs[0].at[:, :, h * D:(h + 1) * D])
+              for h in range(HEADS)]
+    pieces += list(zip(ins[1:], held[1:], outs[1:]))
+    reads = [pltpu.make_async_copy(src, mid, sem_in.at[i])
+             for i, (src, mid, _) in enumerate(pieces)]
+    writes = [pltpu.make_async_copy(mid, dst, sem_out.at[i])
+              for i, (_, mid, dst) in enumerate(pieces)]
+    for copy in reads:
         copy.start()
-    for copy in copies:
+    for read, write in zip(reads, writes):
+        read.wait()
+        write.start()
+    for copy in writes:
         copy.wait()
 
 
@@ -365,15 +372,16 @@
     SYS, CTX = SL * levels, CL * levels
     M = -(-HEADS * T // 128) * 128
     OWN = levels * T
+    PAIR = 2 if R % 2 == 0 else 1
     N = SYS + CTX + OWN
     SH = 2 * (SL + C * CL)
     rq = SL // reqs
     vmem = pl.BlockSpec(memory_space=pltpu.VMEM)
-    any_place = pl.BlockSpec(memory_space=pl.ANY)
+    hbm = pl.BlockSpec(memory_space=pltpu.HBM)
     dma = pltpu.SemaphoreType.DMA
     V = pltpu.VMEM
     outs = pl.pallas_call(
-        functools.partial(kernel, levels, reqs, T, R, SYS, CTX, C, M),
+        functools.partial(kernel, levels, reqs, T, R, SYS, CTX, C, M, PAIR),
         out_shape=(
             jax.ShapeDtypeStruct((HEADS, T * R, D), F32),
             jax.ShapeDtypeStruct((rq, D), F32),
@@ -383,8 +391,8 @@
             jax.ShapeDtypeStruct((T * R, D), F32),
             jax.ShapeDtypeStruct((T * R, D), F32),
         ),
-        in_specs=[any_place] * 11,
-        out_specs=(any_place,) + (vmem,) * 6,
+        in_specs=[hbm] * 11,
+        out_specs=(hbm,) + (vmem,) * 6,
         scratch_shapes=[
             V((T, R, HEADS * D), BF16),
             V((T, R, HEADS * D), BF16),
@@ -401,12 +409,14 @@
             V((2, T * R, D), F32),
             V((R, 2, OWN, D), BF16),
             V((levels, SH, D), BF16),
-            V((2, CTX, D), BF16),
+            V((PAIR, 2, N, D), BF16),
             V((R, M, D), BF16),
             V((R, M, D), BF16),
-            V((N, M), F32),
-            V((N, M), F32),
-            V((2, OWN, D), F32),
+            V((PAIR, N, M), F32),
+            V((PAIR, N, M), F32),
+            V((PAIR, N, M), BF16),
+            V((PAIR, N, M), BF16),
+            V((PAIR, 2, OWN, D), F32),
             V((R, 2, T, D), F32),
             V((R, levels, 2, T, D), BF16),
             V((R, levels, 2, T, D), BF16),
@@ -438,9 +448,9 @@
     return pl.pallas_call(
         write_out,
         out_shape=tuple(jax.ShapeDtypeStruct(shape, F32) for shape in shapes),
-        in_specs=[any_place] * 7,
-        out_specs=(any_place,) * 7,
-        scratch_shapes=[dma((HEADS + 6,))],
+        in_specs=[hbm] * 7,
+        out_specs=(hbm,) * 7,
+        scratch_shapes=[V(a.shape, F32) for a in finals] + [dma((HEADS + 6,)), dma((HEADS + 6,))],
         compiler_params=pltpu.CompilerParams(vmem_limit_bytes=56 * 2**20),
     )(*finals)
 

time: 112 us -> 41 us (0.37)
  Pallas kernels: 111 us -> 40.2 us
    pallas_call x1, Pallas kernels: 74.8 us -> 2.6 us  [shards(): pl.pallas_call(write_out, out_shape=tuple((jax.ShapeDtypeStruct(shape, F3...]
    pallas_call x1, Pallas kernels: 36.4 us -> 37.6 us  [shards(): pl.pallas_call(functools.partial(kernel, levels, reqs, T, R, SYS, CTX, C,...]
where the time goes in v3:
time: 41 us; the launch traced here: 40.8 us
  Pallas kernels  40.2 us (98%)
  between operations  0.64 us (2%)
    pallas_call x1, Pallas kernels, shards(): pl.pallas_call(functools.partial(kernel, levels, reqs, T, R, SYS, CTX, C,...  37.6 us
    pallas_call x1, Pallas kernels, shards(): pl.pallas_call(write_out, out_shape=tuple((jax.ShapeDtypeStruct(shape, F3...  2.6 us

profile of v3, /device:TPU:0, one launch (start us, length us, event | category | flops | bytes accessed | tf_op | source)
XLA Modules:
  0.0 40.8 jit_solution(12006051874460170216)
XLA Ops:
  0.6 37.6 %shard_map.162 = (f32[7,512,128]{2,1,0:T(8,128)}, f32[4,128]{1,0:T(4,128)}, f32[4,128]{1,0:T(4,128)}, f32[2,32,128]{2,1,0:T(8,128)}, f32[2,32,128]{2,1,0:T(8,128...) custom-call(bf16[64,8,896]{2,1,0:T(8,128)(2,1)} %q_in.1, bf16[64,8,896]{2,1,0:T(8,128)(2,1)} %g_in.1, ...), custom_call_target="tpu_custom_call" | custom-call | flops 2684354560 | bytes 4587520 | tf_op jit(solution)/shard_map/pallas_call | solution.py:383
  38.2 2.6 %shard_map.163 = (f32[64,8,896]{2,1,0:T(8,128)}, f32[4,128]{1,0:T(4,128)}, f32[4,128]{1,0:T(4,128)}, f32[2,32,128]{2,1,0:T(8,128)}, f32[2,32,128]{2,1,0:T(8,128)...) custom-call(f32[7,64,8,128]{3,2,1,0:T(8,128)} %bitcast.3, f32[4,128]{1,0:T(4,128)} %get-tuple-element.15.refs_1_, ...), custom_call_target="tpu_custom_call" | custom-call | tf_op jit(solution)/shard_map/pallas_call | solution.py:448

commit v4 on v3

--- a/solution.py
+++ b/solution.py
@@ -166,7 +166,7 @@
 
     chunks = []
     for kind, begin, length in (("sys", 0, SYS), ("ctx", SYS, CTX), ("own", SYS + CTX, OWN)):
-        width = min(128, length)
+        width = min(32, length)
         for start in range(0, length, width):
             chunks.append((kind, start, width, slice(begin + start, begin + start + width)))
     row_of_lane = me * T + lax.rem(lax.broadcasted_iota(jnp.int32, (1, M), 1), T)

time: 41 us -> 41 us (level)
  no operation moved by 1% of the time
where the time goes in v4:
time: 41 us; the launch traced here: 40.9 us
  Pallas kernels  40.2 us (98%)
  between operations  0.64 us (2%)
    pallas_call x1, Pallas kernels, shards(): pl.pallas_call(functools.partial(kernel, levels, reqs, T, R, SYS, CTX, C,...  37.6 us
    pallas_call x1, Pallas kernels, shards(): pl.pallas_call(write_out, out_shape=tuple((jax.ShapeDtypeStruct(shape, F3...  2.6 us

profile of v4, /device:TPU:0, one launch (start us, length us, event | category | flops | bytes accessed | tf_op | source)
XLA Modules:
  0.0 40.9 jit_solution(3575915960789902776)
XLA Ops:
  0.6 37.6 %shard_map.162 = (f32[7,512,128]{2,1,0:T(8,128)}, f32[4,128]{1,0:T(4,128)}, f32[4,128]{1,0:T(4,128)}, f32[2,32,128]{2,1,0:T(8,128)}, f32[2,32,128]{2,1,0:T(8,128...) custom-call(bf16[64,8,896]{2,1,0:T(8,128)(2,1)} %q_in.1, bf16[64,8,896]{2,1,0:T(8,128)(2,1)} %g_in.1, ...), custom_call_target="tpu_custom_call" | custom-call | flops 2684354560 | bytes 4587520 | tf_op jit(solution)/shard_map/pallas_call | solution.py:383
  38.3 2.6 %shard_map.163 = (f32[64,8,896]{2,1,0:T(8,128)}, f32[4,128]{1,0:T(4,128)}, f32[4,128]{1,0:T(4,128)}, f32[2,32,128]{2,1,0:T(8,128)}, f32[2,32,128]{2,1,0:T(8,128)...) custom-call(f32[7,64,8,128]{3,2,1,0:T(8,128)} %bitcast.3, f32[4,128]{1,0:T(4,128)} %get-tuple-element.15.refs_1_, ...), custom_call_target="tpu_custom_call" | custom-call | tf_op jit(solution)/shard_map/pallas_call | solution.py:448

commit v5 on v4

--- a/solution.py
+++ b/solution.py
@@ -227,54 +227,51 @@
             ch_s[j, at, :] = chances.astype(BF16)
             sl_s[j, at, :] = (chances * (p_s[j, at, :] - deltas)).astype(BF16)
 
-    def gradients(j, r, chosen):
-        dk = nn(sl_s[j], q_s[r]) * SCALING
-        dv = nn(ch_s[j], g_s[r])
-        for i, grad in ((0, dk), (1, dv)):
+    def send_sums():
+        for b in range(levels):
+            @pl.when(b != me)
+            def _(b=b):
+                for i, base in ((0, K0), (1, V0)):
+                    rows = shared_acc_sys[i, b * SL:(b + 1) * SL]
+                    csend[b, base:base + SL] = rows.astype(BF16)
+                    for c in range(C):
+                        at = base + SL + c * CL
+                        rows = shared_acc_ctx[i, c, b * CL:(b + 1) * CL]
+                        csend[b, at:at + CL] = rows.astype(BF16)
+                sum_copy(b, me).start()
+
+    def one_response(r, last):
+        for b in range(levels):
+            @pl.when(b < me)
+            def _(b=b):
+                kv_copy(r, b, b).wait_recv()
+        chosen, limit = prepare(0, r)
+        roundings(0, *sums(0, maxima(0, limit)))
+        for i, grad in ((0, nn(sl_s[0], q_s[r]) * SCALING), (1, nn(ch_s[0], g_s[r]))):
             shared_acc_sys[i] += grad[:SYS]
             for c in range(C):
                 shared_acc_ctx[i, c] += grad[SYS:SYS + CTX] * chosen[c]
-            own_part[j, i] = grad[SYS + CTX:]
-        dq_rows = jnp.transpose(tn(keys[j, 0], sl_s[j])) * SCALING
+            own_part[0, i] = grad[SYS + CTX:]
+        if last:
+            send_sums()
+        for b in range(levels):
+            @pl.when(b < me)
+            def _(b=b):
+                gsend[r, b] = own_part[0, :, b * T:(b + 1) * T, :].astype(BF16)
+                grad_copy(r, b, me).start()
+        own_grad[r] = own_part[0, :, mine, :]
+        dq_rows = jnp.transpose(tn(keys[0, 0], sl_s[0])) * SCALING
         for h in range(HEADS):
             dq_ref[h, pl.ds(r, T, stride=R), :] = dq_rows[h * T:(h + 1) * T]
 
-    def responses(step, carry):
-        rs = [step * PAIR + j for j in range(PAIR)]
-        for b in range(levels):
-            @pl.when(b < me)
-            def _(b=b):
-                for r in rs:
-                    kv_copy(r, b, b).wait_recv()
-        ready = [prepare(j, r) for j, r in enumerate(rs)]
-        tops = [maxima(j, ready[j][1]) for j in range(PAIR)]
-        for j, r in enumerate(rs):
-            roundings(j, *sums(j, tops[j]))
-        for j, r in enumerate(rs):
-            gradients(j, r, ready[j][0])
-        for j, r in enumerate(rs):
-            own_grad[r] = own_part[j, :, mine, :]
-        for b in range(levels):
-            @pl.when(b < me)
-            def _(b=b):
-                for j, r in enumerate(rs):
-                    gsend[r, b] = own_part[j, :, b * T:(b + 1) * T, :].astype(BF16)
-                    grad_copy(r, b, me).start()
+    def step(r, carry):
+        one_response(r, False)
         return carry
 
-    lax.fori_loop(0, R // PAIR, responses, 0)
+    lax.fori_loop(0, R - 1, step, 0)
+    one_response(R - 1, True)
     dq_copy = pltpu.make_async_copy(dq_ref, dq_out, dq_s)
     dq_copy.start()
-
-    for b in range(levels):
-        @pl.when(b != me)
-        def _(b=b):
-            for which, base in ((0, K0), (1, V0)):
-                csend[b, base:base + SL] = shared_acc_sys[which, b * SL:(b + 1) * SL].astype(BF16)
-                for c in range(C):
-                    at = base + SL + c * CL
-                    csend[b, at:at + CL] = shared_acc_ctx[which, c, b * CL:(b + 1) * CL].astype(BF16)
-            sum_copy(b, me).start()
 
     def finish(r, carry):
         for b in range(levels):
@@ -372,7 +369,7 @@
     SYS, CTX = SL * levels, CL * levels
     M = -(-HEADS * T // 128) * 128
     OWN = levels * T
-    PAIR = 2 if R % 2 == 0 else 1
+    PAIR = 1
     N = SYS + CTX + OWN
     SH = 2 * (SL + C * CL)
     rq = SL // reqs

time: 41 us -> 42 us (1.024)
  Pallas kernels: 40.2 us -> 41.2 us
    pallas_call x1, Pallas kernels: 37.6 us -> 38.6 us  [shards(): pl.pallas_call(functools.partial(kernel, levels, reqs, T, R, SYS, CTX, C,...]
where the time goes in v5:
time: 42 us; the launch traced here: 41.8 us
  Pallas kernels  41.2 us (98%)
  between operations  0.64 us (2%)
    pallas_call x1, Pallas kernels, shards(): pl.pallas_call(functools.partial(kernel, levels, reqs, T, R, SYS, CTX, C,...  38.6 us
    pallas_call x1, Pallas kernels, shards(): pl.pallas_call(write_out, out_shape=tuple((jax.ShapeDtypeStruct(shape, F3...  2.6 us

profile of v5, /device:TPU:0, one launch (start us, length us, event | category | flops | bytes accessed | tf_op | source)
XLA Modules:
  0.0 41.8 jit_solution(18438487791384543027)
XLA Ops:
  0.6 38.6 %shard_map.162 = (f32[7,512,128]{2,1,0:T(8,128)}, f32[4,128]{1,0:T(4,128)}, f32[4,128]{1,0:T(4,128)}, f32[2,32,128]{2,1,0:T(8,128)}, f32[2,32,128]{2,1,0:T(8,128...) custom-call(bf16[64,8,896]{2,1,0:T(8,128)(2,1)} %q_in.1, bf16[64,8,896]{2,1,0:T(8,128)(2,1)} %g_in.1, ...), custom_call_target="tpu_custom_call" | custom-call | flops 2684354560 | bytes 4587520 | tf_op jit(solution)/shard_map/pallas_call | solution.py:380
  39.2 2.6 %shard_map.163 = (f32[64,8,896]{2,1,0:T(8,128)}, f32[4,128]{1,0:T(4,128)}, f32[4,128]{1,0:T(4,128)}, f32[2,32,128]{2,1,0:T(8,128)}, f32[2,32,128]{2,1,0:T(8,128)...) custom-call(f32[7,64,8,128]{3,2,1,0:T(8,128)} %bitcast.3, f32[4,128]{1,0:T(4,128)} %get-tuple-element.15.refs_1_, ...), custom_call_target="tpu_custom_call" | custom-call | tf_op jit(solution)/shard_map/pallas_call | solution.py:445
